TPU v7x, 768 devices: a whole 4x8x12 slice. The times are simulated.
768 devices in a mesh: node: 12 (over z), local: 64 (over y, x, core).
Axes of the slice: x: 4, y: 8, z: 12, core: 2. Of those that a mesh axis runs over, the one named last changes fastest.
Arguments:
- inputs_x: bfloat16 [36864, 2048], P(('node', 'local')), may hold values from -6 to 6
- grad_out: bfloat16 [36864, 2048], P(('node', 'local')), may hold values from -6 to 6
- group_order: int32 [768, 12], P(('node', 'local')), may hold values from 0 to 11, each once within a row
- route_picks: int32 [36864, 1], P(('node', 'local')), may hold values from 0 to 7; in each aligned block of 48 rows (0 to 47, 48 to 95, ...) at most 6 rows name the same one
- gate_weights: bfloat16 [36864, 1], P(('node', 'local')), may hold values from 0.099609375 to 0.69921875
- w_gate: bfloat16 [393216, 512], P(('node', 'local')), may hold values from -0.125 to 0.125
- w_up: bfloat16 [393216, 512], P(('node', 'local')), may hold values from -0.125 to 0.125
- w_down: bfloat16 [393216, 512], P(('node', 'local')), may hold values from -0.1875 to 0.1875
Outputs:
- grad_x: bfloat16 [36864, 2048], P(('node', 'local'))
Inputs may be any that keep to these rules, and one draw needn't show every extreme that they name: `group_order`: every row is a permutation; so each device's tokens pick each node group exactly 4 times. `route_picks`: the 1 numbers of a row differ; in each aligned block of 48 rows (the rows of one device) no number stands in more than 6 rows, and some number stands in exactly 6 rows of some block.
All inputs are finite; a program needn't handle non-finite values.
Results may differ from a plain program's by a relative error of at most 0.0065.
Values may be sent and summed in bfloat16 or wider, within the bound.
A program may use at most 32 MiB of HBM per device.

v0:
```python
import jax
import jax.numpy as jnp
from jax import lax
from jax.sharding import PartitionSpec as P

HSPLIT = 2


def from_partner(value, axis, bit):
    mask = 2**bit
    pairs = [(source, source ^ mask) for source in range(lax.axis_size(axis))]
    return lax.ppermute(value, axis, pairs)


def node_move(payload):
    return lax.all_to_all(payload, "node", split_axis=1, concat_axis=1, tiled=True)


def local_move(payload):
    return lax.all_to_all(payload, "local", split_axis=1, concat_axis=1, tiled=True)


def halves_add(payload, bit_num):
    return from_partner(payload, "local", bit_num)


def partner_copy(payload, bit_num):
    return from_partner(payload, "local", bit_num)


def spread_back(pieces, w_gate, w_up):
    half_width = w_gate.shape[1]
    d_gate = pieces[:, :half_width]
    d_up = pieces[:, half_width : 2 * half_width]
    column_dims = (((1,), (1,)), ((), ()))
    summed = lax.dot_general(d_gate, w_gate, column_dims, preferred_element_type=jnp.float32)
    summed = summed + lax.dot_general(d_up, w_up, column_dims, preferred_element_type=jnp.float32)
    return summed.astype(jnp.bfloat16)


def joined(upper_bit, mine, theirs):
    first_half = jnp.where(upper_bit == 1, theirs, mine)
    second_half = jnp.where(upper_bit == 1, mine, theirs)
    return jnp.concatenate([first_half, second_half], axis=0)


def per_device(inputs_x, grad_out, group_order, route_picks, gate_weights, w_gate, w_up, w_down):
    n_node = lax.axis_size("node")
    n_local = lax.axis_size("local")
    tok_dev, model_width = inputs_x.shape
    rows_in, per_group = route_picks.shape
    cap_group = rows_in // n_node
    groups_tok = rows_in // tok_dev
    d_dev, half_width = w_gate.shape
    d_split = model_width // d_dev
    exp_node = n_local // (HSPLIT * d_split)
    cap_expert = (rows_in * per_group + exp_node - 1) // exp_node
    slot_count = n_local * cap_expert
    full_prec = lax.Precision.HIGHEST
    seq_groups = group_order[0]
    group_ids = jnp.arange(n_node, dtype=jnp.int32)
    position = jnp.sum(
        jnp.where(seq_groups[None, :] == group_ids[:, None], group_ids[None, :], 0), axis=1
    )
    slot_index = jnp.arange(cap_group, dtype=jnp.int32)
    placed = slot_index[None, :] * n_node + position[:, None]
    owner_tok = (placed // groups_tok).reshape(n_node * cap_group)
    stacked = jnp.stack([inputs_x, grad_out])
    outgoing = jnp.take(stacked, owner_tok, axis=1)
    arrived = node_move(outgoing)
    flat_pick = route_picks.reshape(rows_in * per_group)
    expert_ids = jnp.arange(exp_node, dtype=jnp.int32)
    onehot = (flat_pick[:, None] == expert_ids[None, :]).astype(jnp.int32)
    before = jnp.cumsum(onehot, axis=0) - onehot
    slot_rank = jnp.sum(before * onehot, axis=1)
    target = flat_pick * cap_expert + slot_rank
    slot_ids = jnp.arange(exp_node * cap_expert, dtype=jnp.int32)
    slot_match = (
        (target[:, None] == slot_ids[None, :])
        .astype(jnp.float32)
        .reshape(rows_in, per_group, exp_node * cap_expert)
    )
    choose = jnp.sum(slot_match, axis=1)
    weighted = jnp.sum(slot_match * gate_weights.astype(jnp.float32)[:, :, None], axis=1)
    x_disp = jnp.dot(
        choose.T.astype(jnp.bfloat16), arrived[0], preferred_element_type=jnp.float32
    ).astype(jnp.bfloat16)
    dout_disp = jnp.dot(
        weighted.T.astype(jnp.bfloat16), arrived[1], preferred_element_type=jnp.float32
    ).astype(jnp.bfloat16)
    dispatched = jnp.stack([x_disp, dout_disp]).reshape(2, exp_node, cap_expert, d_split, d_dev)
    dispatched = jnp.transpose(dispatched, (0, 1, 3, 2, 4))
    dispatched = jnp.broadcast_to(
        dispatched[:, :, None], (2, exp_node, HSPLIT, d_split, cap_expert, d_dev)
    )
    received = local_move(dispatched.reshape(2, slot_count, d_dev))
    rows_x = received[0]
    rows_dout = received[1]
    partial_value = jnp.concatenate(
        [
            jnp.dot(rows_x, w_gate, preferred_element_type=jnp.float32),
            jnp.dot(rows_x, w_up, preferred_element_type=jnp.float32),
            jnp.dot(rows_dout, w_down, preferred_element_type=jnp.float32),
        ],
        axis=1,
    )
    local_pos = lax.axis_index("local")
    bit_list = list(range(d_split.bit_length() - 1))
    row_share = partial_value
    for bit_num in bit_list:
        half_rows = row_share.shape[0] // 2
        upper_bit = local_pos >> bit_num & 1
        kept_rows = lax.dynamic_slice_in_dim(row_share, upper_bit * half_rows, half_rows, 0)
        given_rows = lax.dynamic_slice_in_dim(row_share, (1 - upper_bit) * half_rows, half_rows, 0)
        row_share = kept_rows + halves_add(given_rows, bit_num)
    pre_gate = row_share[:, :half_width]
    pre_up = row_share[:, half_width : 2 * half_width]
    grad_hid = row_share[:, 2 * half_width :]
    sigmoid_gate = jax.nn.sigmoid(pre_gate)
    d_gate = (grad_hid * pre_up * sigmoid_gate * (1.0 + pre_gate * (1.0 - sigmoid_gate))).astype(
        jnp.bfloat16
    )
    d_up = (grad_hid * pre_gate * sigmoid_gate).astype(jnp.bfloat16)
    pieces = jnp.concatenate([d_gate, d_up], axis=1)
    for bit_num in bit_list[::-1]:
        upper_bit = local_pos >> bit_num & 1
        peer_block = partner_copy(pieces, bit_num)
        pieces = joined(upper_bit, pieces, peer_block)
    contrib = spread_back(pieces, w_gate, w_up)
    returned = local_move(contrib[None])
    term_rows = (
        returned[0]
        .astype(jnp.float32)
        .reshape(exp_node, HSPLIT, d_split, cap_expert, d_dev)
        .sum(axis=1)
    )
    term_rows = jnp.transpose(term_rows, (0, 2, 1, 3)).reshape(exp_node * cap_expert, model_width)
    group_rows = jnp.dot(choose, term_rows, precision=full_prec).astype(jnp.bfloat16)
    arrived_home = node_move(group_rows[None])
    token_ids = jnp.arange(tok_dev, dtype=jnp.int32)
    collect = (token_ids[:, None] == owner_tok[None, :]).astype(jnp.bfloat16)
    grad_x = jnp.dot(collect, arrived_home[0], preferred_element_type=jnp.float32).astype(
        jnp.bfloat16
    )
    return grad_x


def solution(mesh):
    placed = (
        P(("node", "local"), None),
        P(("node", "local"), None),
        P(("node", "local"), None),
        P(("node", "local"), None),
        P(("node", "local"), None),
        P(("node", "local"), None),
        P(("node", "local"), None),
        P(("node", "local"), None),
    )
    return jax.shard_map(
        per_device,
        mesh=mesh,
        in_specs=placed,
        out_specs=P(("node", "local"), None),
        check_vma=False,
    )
```

profile of v0, /device:TPU:6, one launch (start us, length us, event | category | flops | bytes accessed | tf_op | source)
XLA Modules:
  0.0 171.0 jit_solution(4723017459562235705)
XLA Ops:
  0.0 0.8 select_reduce_fusion.1
  1.1 1.2 copy.26
  2.4 1.2 copy.27
  3.6 0.9 pad_maximum_fusion.3
  4.5 1.3 gather_fusion
  5.9 1.2 fusion.14
  7.0 15.2 %all-to-all-start = ((bf16[2,48,2048]{2,0,1:T(2,128)(2,1)}), bf16[2,48,2048]{2,0,1:T(2,128)(2,1)S(1)}, u32[]{:S(2)}, u32[]{:S(2)}) async-start(bf16[2,48,2048]{2,0,1:T(2,128)(2,1)} %fusion.14), calls=%async_computation | async-start | bytes 786432 | tf_op jit(solution)/shard_map/all_to_all | solution.py:16
  22.6 19.4 %all-to-all-done = bf16[2,48,2048]{2,0,1:T(2,128)(2,1)S(1)} async-done(((bf16[2,48,2048]{2,0,1:T(2,128)(2,1)}), bf16[2,48,2048]{2,0,1:T(2,128)(2,1)S(1)}, u32[]{:S(2)}, u32[]{:S(2)}) %all-to-all-start) | async-done | bytes 393248 | tf_op jit(solution)/shard_map/all_to_all | solution.py:16
  42.0 0.5 fusion.41
  42.5 0.3 convolution_convert_fusion.3
  42.9 0.3 convolution_convert_fusion.2
  43.3 0.3 maximum_bitcast_fusion
  43.6 0.4 copy.28
  44.0 1.5 broadcast_in_dim.47
  45.5 10.6 %all-to-all-start.1 = ((bf16[2,384,512]{2,0,1:T(2,128)(2,1)}), bf16[2,384,512]{2,0,1:T(2,128)(2,1)S(1)}, u32[]{:S(2)}, u32[]{:S(2)}) async-start(bf16[2,384,512]{2,0,1:T(2,128)(2,1)} %bitcast.11), calls=%async_computation.1 | async-start | bytes 1572864 | tf_op jit(solution)/shard_map/all_to_all | solution.py:20
  56.1 23.2 %all-to-all-done.1 = bf16[2,384,512]{2,0,1:T(2,128)(2,1)S(1)} async-done(((bf16[2,384,512]{2,0,1:T(2,128)(2,1)}), bf16[2,384,512]{2,0,1:T(2,128)(2,1)S(1)}, u32[]{:S(2)}, u32[]{:S(2)}) %all-to-all-start.1) | async-done | bytes 786464 | tf_op jit(solution)/shard_map/all_to_all | solution.py:20
  79.3 1.1 fusion.40
  80.4 0.4 fusion.10
  80.8 0.6 copy-done.2
  81.5 0.4 fusion.12
  81.8 0.7 copy-done.3
  82.5 0.4 fusion.7
  83.0 1.1 constant_dynamic-slice_fusion
  84.1 1.9 %collective-permute-start = (f32[192,1536]{1,0:T(8,128)}, f32[192,1536]{1,0:T(8,128)}, u32[]{:S(2)}, u32[]{:S(2)}) collective-permute-start(f32[192,1536]{1,0:T(8,128)} %constant_dynamic-slice_fusion), channel_id=1, source_target_pairs={{0,1},{1,0},{2,3},{3,2},{4,5},{5,4},{6,7},{7,6},{8,9},{9,8},{10,11... | collective-permute-start | bytes 3538952 | tf_op jit(solution)/shard_map/ppermute | solution.py:12
  86.1 3.1 %collective-permute-done = f32[192,1536]{1,0:T(8,128)} collective-permute-done((f32[192,1536]{1,0:T(8,128)}, f32[192,1536]{1,0:T(8,128)}, u32[]{:S(2)}, u32[]{:S(2)}) %collective-permute-start) | collective-permute-done | bytes 1179680 | tf_op jit(solution)/shard_map/ppermute | solution.py:12
  89.2 1.4 dynamic-slice_add_fusion
  90.6 1.0 copy-done.1
  91.7 2.7 %collective-permute-start.1 = (f32[96,1536]{1,0:T(8,128)S(1)}, f32[96,1536]{1,0:T(8,128)S(1)}, u32[]{:S(2)}, u32[]{:S(2)}) collective-permute-start(f32[96,1536]{1,0:T(8,128)S(1)} %constant_dynamic-slice_fusion.1), channel_id=1, source_target_pairs={{0,2},{1,3},{2,0},{3,1},{4,6},{5,7},{6,4},{7,5},{8,10},{9,11},{10,... | collective-permute-start | bytes 1769480 | tf_op jit(solution)/shard_map/ppermute | solution.py:12
  94.4 14.5 %collective-permute-done.1 = f32[96,1536]{1,0:T(8,128)S(1)} collective-permute-done((f32[96,1536]{1,0:T(8,128)S(1)}, f32[96,1536]{1,0:T(8,128)S(1)}, u32[]{:S(2)}, u32[]{:S(2)}) %collective-permute-start.1) | collective-permute-done | bytes 589856 | tf_op jit(solution)/shard_map/ppermute | solution.py:12
  108.9 1.1 dynamic-slice_add_fusion.1
  110.2 2.7 %collective-permute-start.2 = (bf16[96,1024]{1,0:T(8,128)(2,1)S(1)}, bf16[96,1024]{1,0:T(8,128)(2,1)S(1)}, u32[]{:S(2)}, u32[]{:S(2)}) collective-permute-start(bf16[96,1024]{1,0:T(8,128)(2,1)S(1)} %pad_maximum_fusion.5), channel_id=1, source_target_pairs={{0,2},{1,3},{2,0},{3,1},{4,6},{5,7},{6,4},{7,5},{8,10},{9,11},{10,... | collective-permute-start | bytes 589832 | tf_op jit(solution)/shard_map/ppermute | solution.py:12
  113.0 5.3 %collective-permute-done.2 = bf16[96,1024]{1,0:T(8,128)(2,1)S(1)} collective-permute-done((bf16[96,1024]{1,0:T(8,128)(2,1)S(1)}, bf16[96,1024]{1,0:T(8,128)(2,1)S(1)}, u32[]{:S(2)}, u32[]{:S(2)}) %collective-permute-start.2) | collective-permute-done | bytes 196640 | tf_op jit(solution)/shard_map/ppermute | solution.py:12
  118.3 2.1 %collective-permute-start.3 = (bf16[192,1024]{1,0:T(8,128)(2,1)S(1)}, bf16[192,1024]{1,0:T(8,128)(2,1)S(1)}, u32[]{:S(2)}, u32[]{:S(2)}) collective-permute-start(bf16[192,1024]{1,0:T(8,128)(2,1)S(1)} %pad_maximum_fusion.4), channel_id=1, source_target_pairs={{0,1},{1,0},{2,3},{3,2},{4,5},{5,4},{6,7},{7,6},{8,9},{9,8},{10,11... | collective-permute-start | bytes 1179656 | tf_op jit(solution)/shard_map/ppermute | solution.py:12
  120.4 1.5 collective-permute-done.3
  122.1 0.4 fusion.5
  122.5 0.4 fusion.2
  123.0 0.6 copy.65
  123.6 0.5 broadcast.148
  124.1 3.0 %reduce.2 = bf16[384,512]{1,0:T(8,128)(2,1)S(1)} reduce(bf16[384,1,512]{2,1,0:T(2,128)(2,1)S(1)} %bitcast.64, bf16[]{:T(256)} %broadcast.148), dimensions={1}, to_apply=%bitcast.62.reduce_sub_computation | reduce | bytes 786434
  127.3 20.4 %all_to_all.20 = bf16[64,2,1536]{2,1,0:T(2,128)(2,1)S(1)} all-to-all(bf16[64,2,1536]{2,1,0:T(2,128)(2,1)S(1)} %reshape.167), channel_id=1, replica_groups=mesh['node'=12,'local'=64] {'local'}, dimensions={0} | all-to-all | bytes 786432 | tf_op jit(solution)/shard_map/all_to_all | solution.py:20
  147.7 0.3 reshape.168
  148.0 2.3 %convert_reduce_fusion = f32[384,512]{1,0:T(8,128)S(1)} fusion(bf16[384,1,512]{2,1,0:T(2,128)(2,1)S(1)} %reshape.168), kind=kLoop, calls=%fused_computation.13 | loop fusion | flops 196608 | bytes 1179648 | tf_op jit(solution)/shard_map/convert_element_type | solution.py:133
  150.6 0.3 copy.30
  151.0 0.4 fusion
  151.3 0.3 copy.66
  151.7 1.8 %reduce.3 = bf16[48,2048]{1,0:T(8,128)(2,1)S(1)} reduce(bf16[48,1,2048]{2,1,0:T(2,128)(2,1)S(1)} %bitcast.68, bf16[]{:T(256)} %broadcast.148), dimensions={1}, to_apply=%bitcast.63.reduce_sub_computation | reduce | bytes 393218
  153.6 16.3 %all_to_all.21 = bf16[12,2,4096]{2,1,0:T(2,128)(2,1)S(1)} all-to-all(bf16[12,2,4096]{2,1,0:T(2,128)(2,1)S(1)} %reshape.169), channel_id=1, replica_groups=mesh['node'=12,'local'=64] {'node'}, dimensions={0} | all-to-all | bytes 393216 | tf_op jit(solution)/shard_map/all_to_all | solution.py:16
  170.1 0.9 convolution_convert_fusion
  (35 shorter events, 2.4 us)
Async XLA Ops:
  0.0 80.4 %copy-start = (bf16[512,512]{1,0:T(8,128)(2,1)S(1)}, bf16[512,512]{1,0:T(8,128)(2,1)}, u32[]{:S(2)}) copy-start(bf16[512,512]{1,0:T(8,128)(2,1)} %param.14) | copy-start | bytes 1572868
  4.5 17.7 %copy-start.4 = (s32[48,1]{0,1:T(1,128)S(1)}, s32[48,1]{0,1:T(1,128)}, u32[]{:S(2)}) copy-start(s32[48,1]{0,1:T(1,128)} %param.11) | copy-start | bytes 580
  7.0 34.9 %all-to-all-start = ((bf16[2,48,2048]{2,0,1:T(2,128)(2,1)}), bf16[2,48,2048]{2,0,1:T(2,128)(2,1)S(1)}, u32[]{:S(2)}, u32[]{:S(2)}) async-start(bf16[2,48,2048]{2,0,1:T(2,128)(2,1)} %fusion.14), calls=%async_computation | async-start | bytes 786432 | tf_op jit(solution)/shard_map/all_to_all | solution.py:16
  22.5 20.4 %copy-start.5 = (bf16[48,1]{0,1:T(2,128)(2,1)S(1)}, bf16[48,1]{0,1:T(2,128)(2,1)}, u32[]{:S(2)}) copy-start(bf16[48,1]{0,1:T(2,128)(2,1)} %param.12) | copy-start | bytes 292
  45.5 33.8 %all-to-all-start.1 = ((bf16[2,384,512]{2,0,1:T(2,128)(2,1)}), bf16[2,384,512]{2,0,1:T(2,128)(2,1)S(1)}, u32[]{:S(2)}, u32[]{:S(2)}) async-start(bf16[2,384,512]{2,0,1:T(2,128)(2,1)} %bitcast.11), calls=%async_computation.1 | async-start | bytes 1572864 | tf_op jit(solution)/shard_map/all_to_all | solution.py:20
  80.4 1.0 copy-start.2
  81.5 1.0 copy-start.3
  84.1 5.1 %collective-permute-start = (f32[192,1536]{1,0:T(8,128)}, f32[192,1536]{1,0:T(8,128)}, u32[]{:S(2)}, u32[]{:S(2)}) collective-permute-start(f32[192,1536]{1,0:T(8,128)} %constant_dynamic-slice_fusion), channel_id=1, source_target_pairs={{0,1},{1,0},{2,3},{3,2},{4,5},{5,4},{6,7},{7,6},{8,9},{9,8},{10,11... | collective-permute-start | bytes 3538952 | tf_op jit(solution)/shard_map/ppermute | solution.py:12
  90.6 1.0 copy-start.1
  91.7 17.3 %collective-permute-start.1 = (f32[96,1536]{1,0:T(8,128)S(1)}, f32[96,1536]{1,0:T(8,128)S(1)}, u32[]{:S(2)}, u32[]{:S(2)}) collective-permute-start(f32[96,1536]{1,0:T(8,128)S(1)} %constant_dynamic-slice_fusion.1), channel_id=1, source_target_pairs={{0,2},{1,3},{2,0},{3,1},{4,6},{5,7},{6,4},{7,5},{8,10},{9,11},{10,... | collective-permute-start | bytes 1769480 | tf_op jit(solution)/shard_map/ppermute | solution.py:12
  110.2 8.0 %collective-permute-start.2 = (bf16[96,1024]{1,0:T(8,128)(2,1)S(1)}, bf16[96,1024]{1,0:T(8,128)(2,1)S(1)}, u32[]{:S(2)}, u32[]{:S(2)}) collective-permute-start(bf16[96,1024]{1,0:T(8,128)(2,1)S(1)} %pad_maximum_fusion.5), channel_id=1, source_target_pairs={{0,2},{1,3},{2,0},{3,1},{4,6},{5,7},{6,4},{7,5},{8,10},{9,11},{10,... | collective-permute-start | bytes 589832 | tf_op jit(solution)/shard_map/ppermute | solution.py:12
  118.3 3.6 %collective-permute-start.3 = (bf16[192,1024]{1,0:T(8,128)(2,1)S(1)}, bf16[192,1024]{1,0:T(8,128)(2,1)S(1)}, u32[]{:S(2)}, u32[]{:S(2)}) collective-permute-start(bf16[192,1024]{1,0:T(8,128)(2,1)S(1)} %pad_maximum_fusion.4), channel_id=1, source_target_pairs={{0,1},{1,0},{2,3},{3,2},{4,5},{5,4},{6,7},{7,6},{8,9},{9,8},{10,11... | collective-permute-start | bytes 1179656 | tf_op jit(solution)/shard_map/ppermute | solution.py:12
where the time goes:
time: 173 us; the launch traced here: 171 us
  waiting for transfers between devices  67 us (39%)
  blocking collectives  36.7 us (21%)
  starting transfers between devices  35.3 us (20%)
  local copies, waits for them, and re-layouts  14 us (8%)
  other arithmetic  13.9 us (8%)
  matrix products  3.71 us (2%)
    ppermute x4, waiting for transfers between devices, from_partner(): return lax.ppermute(value, axis, pairs)  24.4 us
    all_to_all x1, waiting for transfers between devices, local_move(): lax.all_to_all(payload, 'local', split_axis=1, concat_axis=1, tiled=True)  23.2 us
    all_to_all x1, blocking collectives, local_move(): lax.all_to_all(payload, 'local', split_axis=1, concat_axis=1, tiled=True)  20.4 us
    all_to_all x1, waiting for transfers between devices, node_move(): lax.all_to_all(payload, 'node', split_axis=1, concat_axis=1, tiled=True)  19.4 us
    all_to_all x1, blocking collectives, node_move(): lax.all_to_all(payload, 'node', split_axis=1, concat_axis=1, tiled=True)  16.3 us
    all_to_all x1, starting transfers between devices, node_move(): lax.all_to_all(payload, 'node', split_axis=1, concat_axis=1, tiled=True)  15.2 us
    all_to_all x1, starting transfers between devices, local_move(): lax.all_to_all(payload, 'local', split_axis=1, concat_axis=1, tiled=True)  10.6 us
    ppermute x4, starting transfers between devices, from_partner(): return lax.ppermute(value, axis, pairs)  9.51 us
  transfers between devices with their start and end apart: 6, of which 6 were waited for; matrix products, arithmetic and copies ran while one was open for 0% of the time, Pallas kernels for 0%

commit v1 on v0

v1 whole, which is shorter than its diff:
```python
import jax
import jax.numpy as jnp
from jax import lax
from jax.experimental import pallas as pl
from jax.experimental.pallas import tpu as pltpu
from jax.sharding import PartitionSpec as P

MESH = pl.DeviceIdType.MESH
BF16 = jnp.bfloat16
F32 = jnp.float32
I32 = jnp.int32

NZ, NY, NX = 12, 8, 4
TOK = 48
CAP_G, CAP_E = 4, 6
LT = 8
LANES = 128
ROWS = TOK * LT
HALF = 512
PLANE = NY * NX


def one_hot(key):
    rows = lax.broadcasted_iota(I32, (ROWS, ROWS), 0)
    return jnp.where(rows == key, 1.0, 0.0).astype(BF16)


def reorder(matrix, value):
    return jnp.dot(matrix, value, preferred_element_type=F32).astype(BF16)


def drain(ref, sem):
    pltpu.make_async_copy(ref, ref, sem).wait()


def kernel(
    order_ref, picks_ref, gates_ref, x_hbm, y_hbm, wg_hbm, wu_hbm, wd_hbm, out_ref,
    rows_in, zsend, zrecv, ysend, yrecv, lhs, wbuf, part, part_out, part_in, rsend, rrecv, stage,
    bsend, brecv, p_grp, p_exp, p_expw, p_mat, p_mat_t, p_exp_t, p_grp_t,
    in_sem, w_sem, ws_sem, wr_sem, zs_sem, zr_sem, ys_sem, yr_sem, ps_sem, pr_sem, rs_sem, rr_sem, bs_sem, br_sem,
):
    node = lax.axis_index("node")
    local = lax.axis_index("local")
    core = lax.rem(local, 2)
    my_x = lax.rem(lax.div(local, 2), NX)
    my_y = lax.div(local, 2 * NX)
    here = my_y * NX + my_x
    my_h, my_k = lax.div(my_x, 2), lax.rem(my_x, 2)

    def place(y, x):
        return (node, (y * NX + x) * 2 + core)

    def plane_peer(step):
        spot = lax.rem(here + step, PLANE)
        return lax.div(spot, NX), lax.rem(spot, NX)

    barrier = pltpu.get_barrier_semaphore()

    @pl.loop(1, NZ)
    def _(step):
        pl.semaphore_signal(
            barrier, inc=1, device_id=(lax.rem(node + step, NZ), local), device_id_type=MESH
        )

    @pl.loop(1, PLANE)
    def _(step):
        y, x = plane_peer(step)
        pl.semaphore_signal(barrier, inc=1, device_id=place(y, x), device_id_type=MESH)

    twin = (node, local + 1 - 2 * core)
    pl.semaphore_signal(barrier, inc=1, device_id=twin, device_id_type=MESH)

    load_x = pltpu.make_async_copy(x_hbm, rows_in.at[0], in_sem.at[0])
    load_y = pltpu.make_async_copy(y_hbm, rows_in.at[1], in_sem.at[1])
    load_x.start()
    load_y.start()
    loads_w = [
        pltpu.make_async_copy(w, wbuf.at[m, core], w_sem.at[m])
        for m, w in enumerate((wg_hbm, wu_hbm, wd_hbm))
    ]
    for load in loads_w:
        load.start()

    lane = lax.broadcasted_iota(I32, (1, ROWS), 1)
    tok_b, tok_t = lax.div(lane, TOK), lax.rem(lane, TOK)
    turn = lax.rem(tok_t, NZ)
    group = jnp.zeros((1, ROWS), I32)
    for k in range(NZ):
        group = jnp.where(turn == k, order_ref[0, k], group)
    p_grp[...] = one_hot(group * (LT * CAP_G) + tok_b * CAP_G + lax.div(tok_t, NZ))

    def pack(arr):
        for b in range(LT):
            for f in range(2):
                stage[arr, b * TOK : (b + 1) * TOK, f * LANES : (f + 1) * LANES] = rows_in[
                    arr, :, (f * LT + b) * LANES : (f * LT + b + 1) * LANES
                ]
        zsend[arr] = reorder(p_grp[...], stage[arr]).reshape(NZ, LT * CAP_G, 2 * LANES)

    def start_z(src, dst, s_sem, r_sem):
        @pl.loop(1, NZ)
        def _(step):
            g = lax.rem(node + step, NZ)
            pltpu.make_async_remote_copy(
                src_ref=src.at[g], dst_ref=dst.at[node], send_sem=s_sem, recv_sem=r_sem,
                device_id=(g, local), device_id_type=MESH,
            ).start()

        pltpu.make_async_copy(src.at[node], dst.at[node], r_sem).start()

    load_x.wait()
    pack(0)
    pl.semaphore_wait(barrier, NZ - 1 + PLANE - 1 + 1)
    start_z(zsend.at[0], zrecv.at[0], zs_sem.at[0], zr_sem.at[0])
    load_y.wait()
    pack(1)
    start_z(zsend.at[1], zrecv.at[1], zs_sem.at[1], zr_sem.at[1])

    sends_w = [
        pltpu.make_async_remote_copy(
            src_ref=w, dst_ref=wbuf.at[m, core], send_sem=ws_sem.at[m], recv_sem=wr_sem.at[m],
            device_id=twin, device_id_type=MESH,
        )
        for m, w in enumerate((wg_hbm, wu_hbm, wd_hbm))
    ]
    for send in sends_w:
        send.start()

    picks = picks_ref[...].astype(F32)
    row48 = lax.broadcasted_iota(I32, (TOK, TOK), 0)
    col48 = lax.broadcasted_iota(I32, (TOK, TOK), 1)
    picks_lane = jnp.sum(jnp.where(row48 == col48, picks, 0.0), axis=0, keepdims=True)
    same = (picks == picks_lane) & (col48 < row48)
    rank = jnp.sum(jnp.where(same, 1.0, 0.0), axis=1, keepdims=True)
    grp_n, grp_b, grp_c = lax.div(lane, LT * CAP_G), lax.rem(lax.div(lane, CAP_G), LT), lax.rem(lane, CAP_G)
    row_id = lax.broadcasted_iota(I32, (TOK, ROWS), 0)
    mine = row_id == grp_n * CAP_G + grp_c
    slot_key = jnp.sum(jnp.where(mine, picks * (LT * CAP_E) + rank, 0.0), axis=0, keepdims=True).astype(I32)
    slot_key = slot_key + grp_b * CAP_E
    gate = jnp.sum(jnp.where(mine, gates_ref[...].astype(F32), 0.0), axis=0, keepdims=True)
    p_exp[...] = one_hot(slot_key)
    rows2d = lax.broadcasted_iota(I32, (ROWS, ROWS), 0)
    p_expw[...] = jnp.where(rows2d == slot_key, gate, 0.0).astype(BF16)
    exp_e, exp_b, exp_r = (
        lax.div(lane, LT * CAP_E), lax.rem(lax.div(lane, CAP_E), LT), lax.rem(lane, CAP_E),
    )
    p_mat[...] = one_hot(exp_b * TOK + exp_e * CAP_E + exp_r)
    mat_b, mat_y, mat_r = (
        lax.div(lane, TOK), lax.div(lax.rem(lane, TOK), CAP_E), lax.rem(lane, CAP_E),
    )
    p_mat_t[...] = one_hot(mat_y * (LT * CAP_E) + mat_b * CAP_E + mat_r)

    def start_plane(pick_src, pick_dst, own_src, own_dst, s_sem, r_sem):
        @pl.loop(1, PLANE)
        def _(step):
            y, x = plane_peer(step)
            pltpu.make_async_remote_copy(
                src_ref=pick_src(y, x), dst_ref=pick_dst, send_sem=s_sem, recv_sem=r_sem,
                device_id=place(y, x), device_id_type=MESH,
            ).start()

        pltpu.make_async_copy(own_src, own_dst, r_sem).start()

    def dispatch(arr, matrix):
        drain(zrecv.at[arr], zr_sem.at[arr])
        sorted_rows = reorder(matrix[...], zrecv[arr].reshape(ROWS, 2 * LANES))
        for f in range(2):
            ysend[arr, f] = sorted_rows[:, f * LANES : (f + 1) * LANES].reshape(NY, LT * CAP_E, LANES)
        start_plane(
            lambda y, x: ysend.at[arr, lax.rem(x, 2), y], yrecv.at[arr, my_x, my_y],
            ysend.at[arr, my_k, my_y], yrecv.at[arr, my_x, my_y], ys_sem.at[arr], yr_sem.at[arr],
        )

    dispatch(0, p_exp)
    dispatch(1, p_expw)

    wanted = lax.broadcasted_iota(I32, (TOK, ROWS), 0).astype(F32)
    slot_of_row = (picks * CAP_E + rank).astype(I32)
    here48 = slot_of_row == exp_e * CAP_E + exp_r
    source = jnp.sum(jnp.where(here48, wanted, 0.0), axis=0, keepdims=True).astype(I32)
    p_exp_t[...] = one_hot(
        lax.div(source, CAP_G) * (LT * CAP_G) + exp_b * CAP_G + lax.rem(source, CAP_G)
    )
    position = jnp.zeros((1, ROWS), I32)
    for k in range(NZ):
        position = jnp.where(grp_n == order_ref[0, k], k, position)
    p_grp_t[...] = one_hot(grp_b * TOK + grp_c * NZ + position)

    def gather_rows(arr):
        drain(yrecv.at[arr], yr_sem.at[arr])
        for pair in range(NX // 2):
            value = jnp.concatenate(
                [yrecv[arr, 2 * pair + i].reshape(ROWS, LANES) for i in range(2)], axis=1
            )
            ordered = reorder(p_mat[...], value)
            for i in range(2):
                for b in range(LT):
                    lhs[arr, (2 * pair + i) * TOK : (2 * pair + i + 1) * TOK, b * LANES : (b + 1) * LANES] = (
                        ordered[b * TOK : (b + 1) * TOK, i * LANES : (i + 1) * LANES]
                    )

    partner = place(my_y, my_x + 1 - 2 * my_k)

    def part_copy(m):
        return pltpu.make_async_remote_copy(
            src_ref=part_out.at[m], dst_ref=part_in.at[m], send_sem=ps_sem.at[m], recv_sem=pr_sem.at[m],
            device_id=partner, device_id_type=MESH,
        )

    def project(arr, m):
        value = jnp.dot(lhs[arr], wbuf[m].reshape(2 * HALF, HALF), preferred_element_type=F32)
        part[m] = value
        part_out[m] = value.astype(BF16)
        part_copy(m).start()

    def weights_ready(m):
        loads_w[m].wait()
        sends_w[m].wait_recv()

    gather_rows(0)
    for m in range(2):
        weights_ready(m)
        project(0, m)
    gather_rows(1)
    weights_ready(2)
    project(1, 2)

    for m in range(3):
        part_copy(m).wait_recv()
    pre_gate = part[0] + part_in[0].astype(F32)
    pre_up = part[1] + part_in[1].astype(F32)
    grad_hid = part[2] + part_in[2].astype(F32)
    sig = jax.nn.sigmoid(pre_gate)
    d_gate = (grad_hid * pre_up * sig * (1.0 + pre_gate * (1.0 - sig))).astype(BF16)
    d_up = (grad_hid * pre_gate * sig).astype(BF16)
    dims = (((1,), (1,)), ((), ()))
    contrib = lax.dot_general(d_gate, wbuf[0].reshape(2 * HALF, HALF), dims, preferred_element_type=F32)
    contrib = contrib + lax.dot_general(
        d_up, wbuf[1].reshape(2 * HALF, HALF), dims, preferred_element_type=F32
    )
    contrib = contrib.astype(BF16)
    for pair in range(NX // 2):
        for i in range(2):
            for b in range(LT):
                stage[pair, b * TOK : (b + 1) * TOK, i * LANES : (i + 1) * LANES] = contrib[
                    (2 * pair + i) * TOK : (2 * pair + i + 1) * TOK, b * LANES : (b + 1) * LANES
                ]
        ordered = reorder(p_mat_t[...], stage[pair])
        for i in range(2):
            rsend[(2 * pair + i) * NY : (2 * pair + i + 1) * NY] = ordered[
                :, i * LANES : (i + 1) * LANES
            ].reshape(NY, LT * CAP_E, LANES)
    start_plane(
        lambda y, x: rsend.at[x * NY + y], rrecv.at[my_h, my_k, my_y],
        rsend.at[my_x * NY + my_y], rrecv.at[my_h, my_k, my_y], rs_sem, rr_sem,
    )
    drain(rrecv, rr_sem)
    home = jnp.concatenate(
        [
            (rrecv[0, f].astype(F32) + rrecv[1, f].astype(F32)).astype(BF16).reshape(ROWS, LANES)
            for f in range(2)
        ],
        axis=1,
    )
    bsend[...] = reorder(p_exp_t[...], home).reshape(NZ, LT * CAP_G, 2 * LANES)
    start_z(bsend, brecv, bs_sem, br_sem)
    drain(brecv, br_sem)
    result = reorder(p_grp_t[...], brecv[...].reshape(ROWS, 2 * LANES))
    for f in range(2):
        for b in range(LT):
            out_ref[:, (f * LT + b) * LANES : (f * LT + b + 1) * LANES] = result[
                b * TOK : (b + 1) * TOK, f * LANES : (f + 1) * LANES
            ]

    sent_z = zsend.at[0, pl.ds(0, NZ - 1)]
    drain(sent_z, zs_sem.at[0])
    drain(sent_z, zs_sem.at[1])
    drain(bsend.at[pl.ds(0, NZ - 1)], bs_sem)
    for send in sends_w:
        send.wait_send()
    for m in range(3):
        part_copy(m).wait_send()
    for sem in (ys_sem.at[0], ys_sem.at[1], rs_sem):
        drain(rsend.at[pl.ds(0, PLANE - 1)], sem)


def per_device(inputs_x, grad_out, group_order, route_picks, gate_weights, w_gate, w_up, w_down):
    vmem = pl.BlockSpec(memory_space=pltpu.VMEM)
    hbm = pl.BlockSpec(memory_space=pl.ANY)
    square = pltpu.VMEM((ROWS, ROWS), BF16)
    dma = pltpu.SemaphoreType.DMA
    return pl.pallas_call(
        kernel,
        out_shape=jax.ShapeDtypeStruct(inputs_x.shape, BF16),
        in_specs=[pl.BlockSpec(memory_space=pltpu.SMEM), vmem, vmem] + [hbm] * 5,
        out_specs=vmem,
        scratch_shapes=[
            pltpu.VMEM((2, TOK, 2 * LT * LANES), BF16),
            pltpu.VMEM((2, NZ, LT * CAP_G, 2 * LANES), BF16),
            pltpu.VMEM((2, NZ, LT * CAP_G, 2 * LANES), BF16),
            pltpu.VMEM((2, 2, NY, LT * CAP_E, LANES), BF16),
            pltpu.VMEM((2, NX, NY, LT * CAP_E, LANES), BF16),
            pltpu.VMEM((2, NX * TOK, LT * LANES), BF16),
            pltpu.VMEM((3, 2, HALF, HALF), BF16),
            pltpu.VMEM((3, NX * TOK, HALF), F32),
            pltpu.VMEM((3, NX * TOK, HALF), BF16),
            pltpu.VMEM((3, NX * TOK, HALF), BF16),
            pltpu.VMEM((PLANE, LT * CAP_E, LANES), BF16),
            pltpu.VMEM((2, 2, NY, LT * CAP_E, LANES), BF16),
            pltpu.VMEM((2, ROWS, 2 * LANES), BF16),
            pltpu.VMEM((NZ, LT * CAP_G, 2 * LANES), BF16),
            pltpu.VMEM((NZ, LT * CAP_G, 2 * LANES), BF16),
            square, square, square, square, square, square, square,
            dma((2,)), dma((3,)), dma((3,)), dma((3,)),
            dma((2,)), dma((2,)), dma((2,)), dma((2,)),
            dma((3,)), dma((3,)), dma(()), dma(()), dma(()), dma(()),
        ],
        compiler_params=pltpu.CompilerParams(
            collective_id=0, has_side_effects=True, vmem_limit_bytes=40 * 2**20
        ),
    )(group_order, route_picks, gate_weights, inputs_x, grad_out, w_gate, w_up, w_down)


def solution(mesh):
    placed = P(("node", "local"), None)
    return jax.shard_map(
        per_device, mesh=mesh, in_specs=(placed,) * 8, out_specs=placed, check_vma=False
    )
```

time: 173 us -> 84.4 us (0.49)
  Pallas kernels: 0 us -> 77 us
  waiting for transfers between devices: 67 us -> 0 us
  blocking collectives: 36.7 us -> 0 us
  starting transfers between devices: 35.3 us -> 0 us
  other arithmetic: 13.9 us -> 0 us
  local copies, waits for them, and re-layouts: 14 us -> 7.08 us
  matrix products: 3.71 us -> 0 us
    pallas_call x0 -> x1, Pallas kernels: none -> 77 us  [per_device(): pl.pallas_call(kernel, out_shape=jax.ShapeDtypeStruct(inputs_x.shape, BF1...]
    all_to_all x2 -> x0, waiting for transfers between devices: 42.6 us -> none  [the longest x1 23.2 us: local_move(): lax.all_to_all(payload, 'local', split_axis=1, concat_axis=1, tiled=True)]
    all_to_all x2 -> x0, blocking collectives: 36.7 us -> none  [the longest x1 20.4 us: local_move(): lax.all_to_all(payload, 'local', split_axis=1, concat_axis=1, tiled=True)]
    all_to_all x2 -> x0, starting transfers between devices: 25.8 us -> none  [the longest x1 15.2 us: node_move(): lax.all_to_all(payload, 'node', split_axis=1, concat_axis=1, tiled=True)]
    ppermute x4 -> x0, waiting for transfers between devices: 24.4 us -> none  [from_partner(): return lax.ppermute(value, axis, pairs)]
    ppermute x4 -> x0, starting transfers between devices: 9.51 us -> none  [from_partner(): return lax.ppermute(value, axis, pairs)]
    unnamed x2 -> x0, other arithmetic: 4.78 us -> none
    dot_general x9 -> x0, matrix products: 3.71 us -> none  [the longest x1 0.92 us: per_device(): jnp.dot(collect, arrived_home[0], preferred_element_type=jnp.float32)]
  transfers between devices with their start and end apart: 6 -> 0, of which waited for: 6 -> 0; matrix products, arithmetic and copies ran while one was open for 0% -> 0% of each run, Pallas kernels for 0% -> 0%
where the time goes in v1:
time: 84.4 us; the launch traced here: 84.1 us
  Pallas kernels  77 us (91%)
  local copies, waits for them, and re-layouts  7.08 us (8%)
    pallas_call x1, Pallas kernels, per_device(): pl.pallas_call(kernel, out_shape=jax.ShapeDtypeStruct(inputs_x.shape, BF1...  77 us
    unnamed x17, local copies, waits for them, and re-layouts  7.08 us

profile of v1, /device:TPU:6, one launch (start us, length us, event | category | flops | bytes accessed | tf_op | source)
XLA Modules:
  0.0 84.1 jit_solution(13289182655048552157)
XLA Ops:
  0.0 0.0 copy-start.6
  0.0 0.8 copy.10.gates_ref
  0.8 0.0 copy-done.6
  0.8 0.0 copy-start.5
  0.8 0.1 copy.9.picks_ref
  0.9 0.6 copy-done.5
  1.4 0.0 copy-start
  1.4 1.0 %copy-done = bf16[512,512]{1,0:T(8,128)(2,1)S(1)} copy-done((bf16[512,512]{1,0:T(8,128)(2,1)S(1)}, bf16[512,512]{1,0:T(8,128)(2,1)}, u32[]{:S(2)}) %copy-start) | copy-done | bytes 524312
  2.5 0.0 copy-start.1
  2.5 1.0 %copy-done.1 = bf16[512,512]{1,0:T(8,128)(2,1)S(1)} copy-done((bf16[512,512]{1,0:T(8,128)(2,1)S(1)}, bf16[512,512]{1,0:T(8,128)(2,1)}, u32[]{:S(2)}) %copy-start.1) | copy-done | bytes 524312
  3.5 0.0 copy-start.2
  3.5 1.0 %copy-done.2 = bf16[512,512]{1,0:T(8,128)(2,1)S(1)} copy-done((bf16[512,512]{1,0:T(8,128)(2,1)S(1)}, bf16[512,512]{1,0:T(8,128)(2,1)}, u32[]{:S(2)}) %copy-start.2) | copy-done | bytes 524312
  4.6 0.0 copy-start.3
  4.6 0.9 %copy-done.3 = bf16[48,2048]{1,0:T(8,128)(2,1)S(1)} copy-done((bf16[48,2048]{1,0:T(8,128)(2,1)S(1)}, bf16[48,2048]{1,0:T(8,128)(2,1)}, u32[]{:S(2)}) %copy-start.3) | copy-done | bytes 196632
  5.5 0.0 copy-start.4
  5.5 0.9 %copy-done.4 = bf16[48,2048]{1,0:T(8,128)(2,1)S(1)} copy-done((bf16[48,2048]{1,0:T(8,128)(2,1)S(1)}, bf16[48,2048]{1,0:T(8,128)(2,1)}, u32[]{:S(2)}) %copy-start.4) | copy-done | bytes 196632
  6.4 77.0 %shard_map.82 = bf16[48,2048]{1,0:T(8,128)(2,1)S(1)} custom-call(s32[1,12]{1,0:T(1,128)S(1)} %copy-done.5, s32[48,1]{1,0:T(8,128)S(1)} %copy.9.picks_ref, bf16[48,1]{1,0:T(8,128)(2,1)S(1)} %copy.10.gates_ref, bf16[48,2048]{1,0:T(8,128)(2,1)S(1)} %copy-done.3, bf16[48,2048]{1,0:T(8,128)(2,1)S(1)} %copy-done.4, bf16[512,512]{1,0:T(8,128)(2,1)S(1)} %copy-done, ...), custom_call_target="tpu_custom_call" | custom-call | tf_op jit(solution)/shard_map/pallas_call | solution.py:292
  83.4 0.7 copy.12
Async XLA Ops:
  0.0 0.8 copy-start.6
  0.8 0.7 copy-start.5
  1.4 1.0 %copy-start = (bf16[512,512]{1,0:T(8,128)(2,1)S(1)}, bf16[512,512]{1,0:T(8,128)(2,1)}, u32[]{:S(2)}) copy-start(bf16[512,512]{1,0:T(8,128)(2,1)} %wg_hbm.1) | copy-start | bytes 1572868
  2.5 1.0 %copy-start.1 = (bf16[512,512]{1,0:T(8,128)(2,1)S(1)}, bf16[512,512]{1,0:T(8,128)(2,1)}, u32[]{:S(2)}) copy-start(bf16[512,512]{1,0:T(8,128)(2,1)} %wu_hbm.1) | copy-start | bytes 1572868
  3.5 1.0 %copy-start.2 = (bf16[512,512]{1,0:T(8,128)(2,1)S(1)}, bf16[512,512]{1,0:T(8,128)(2,1)}, u32[]{:S(2)}) copy-start(bf16[512,512]{1,0:T(8,128)(2,1)} %wd_hbm.1) | copy-start | bytes 1572868
  4.6 0.9 %copy-start.3 = (bf16[48,2048]{1,0:T(8,128)(2,1)S(1)}, bf16[48,2048]{1,0:T(8,128)(2,1)}, u32[]{:S(2)}) copy-start(bf16[48,2048]{1,0:T(8,128)(2,1)} %x_hbm.1) | copy-start | bytes 589828
  5.5 0.9 %copy-start.4 = (bf16[48,2048]{1,0:T(8,128)(2,1)S(1)}, bf16[48,2048]{1,0:T(8,128)(2,1)}, u32[]{:S(2)}) copy-start(bf16[48,2048]{1,0:T(8,128)(2,1)} %y_hbm.1) | copy-start | bytes 589828

commit v2 on v0

v2 whole, which is shorter than its diff:
```python
import jax
import jax.numpy as jnp
from jax import lax
from jax.experimental import pallas as pl
from jax.experimental.pallas import tpu as pltpu
from jax.sharding import PartitionSpec as P

MESH = pl.DeviceIdType.MESH
BF16 = jnp.bfloat16
F32 = jnp.float32
I32 = jnp.int32

NZ, NY, NX = 12, 8, 4
TOK = 48
CAP_G, CAP_E = 4, 6
LANES = 128
BLK = 8
FB = 4
ROWS = TOK * BLK
HALF = 512
QUART = 256


def one_hot(key):
    rows = lax.broadcasted_iota(I32, (ROWS, ROWS), 0)
    return jnp.where(rows == key, 1.0, 0.0).astype(BF16)


def reorder(matrix, value):
    return jnp.dot(matrix, value, preferred_element_type=F32).astype(BF16)


def column(row, size):
    shape = (size, row.shape[1])
    diag = lax.broadcasted_iota(I32, shape, 0) == lax.broadcasted_iota(I32, shape, 1)
    return jnp.sum(jnp.where(diag, row, 0.0), axis=1, keepdims=True)


def spread(values, index):
    shape = (values.shape[0], index.shape[1])
    hit = lax.broadcasted_iota(I32, shape, 0) == index
    return jnp.sum(jnp.where(hit, values, 0.0), axis=0, keepdims=True)


def drain(ref, sem):
    pltpu.make_async_copy(ref, ref, sem).wait()


def kernel(
    order_hbm, picks_hbm, gates_hbm, x_hbm, y_hbm, wg_hbm, wu_hbm, wd_hbm, out_ref,
    order_ref, picks_ref, gates_ref, rows_in, stage, zsend, zrecv, ysend, yrecv, xsend, xrecv, lhs,
    wbuf, part, part_out, part_in, rsend, rrecv, qsend, qrecv, bsend, brecv,
    p_grp, p_exp, p_expw, p_mat, p_mat_t, p_exp_t, p_grp_t,
    in_sem, wa_sem, wb_sem, wo_sem, ws_sem, wr_sem, zs_sem, zr_sem, ys_sem, yr_sem, xs_sem, xr_sem,
    ps_sem, pr_sem, rs_sem, rr_sem, qs_sem, qr_sem, bs_sem, br_sem,
):
    node = lax.axis_index("node")
    local = lax.axis_index("local")
    core = lax.rem(local, 2)
    my_x = lax.rem(lax.div(local, 2), NX)
    my_y = lax.div(local, 2 * NX)
    my_h, my_k = lax.div(my_x, 2), lax.rem(my_x, 2)

    def place(y, x):
        return (node, (y * NX + x) * 2 + core)

    z_peers = [lax.rem(node + step, NZ) for step in (6, 5, 7, 4, 8, 3, 9, 2, 10, 1, 11)]
    y_peers = [lax.rem(my_y + step, NY) for step in (4, 3, 5, 2, 6, 1, 7)]
    x_peers = [lax.rem(my_x + step, NX) for step in (2, 1, 3)]
    twin = (node, local + 1 - 2 * core)

    load_x = pltpu.make_async_copy(x_hbm, rows_in.at[0], in_sem.at[0])
    load_y = pltpu.make_async_copy(y_hbm, rows_in.at[1], in_sem.at[1])
    small = [
        pltpu.make_async_copy(src, dst, in_sem.at[2 + i])
        for i, (src, dst) in enumerate(
            ((order_hbm, order_ref), (picks_hbm, picks_ref), (gates_hbm, gates_ref))
        )
    ]
    small[0].start()
    load_x.start()
    load_y.start()
    small[1].start()
    small[2].start()

    barrier = pltpu.get_barrier_semaphore()

    def greet(device):
        pl.semaphore_signal(barrier, inc=1, device_id=device, device_id_type=MESH)

    for z in z_peers:
        greet((z, local))
    for y in y_peers:
        greet(place(y, my_x))
    for x in x_peers:
        greet(place(my_y, x))
    greet(twin)

    lane = lax.broadcasted_iota(I32, (1, ROWS), 1)
    tok_k, tok_t = lax.div(lane, TOK), lax.rem(lane, TOK)
    small[0].wait()
    order = column(order_ref[...].astype(F32), 16)
    group = spread(order, lax.rem(tok_t, NZ)).astype(I32)
    p_grp[...] = one_hot(group * (BLK * CAP_G) + tok_k * CAP_G + lax.div(tok_t, NZ))

    def feature(f, s, b):
        start = f * 2 * HALF + s * HALF + b * LANES
        return slice(start, start + LANES)

    def blocks():
        return [(f, b) for f in range(2) for b in range(FB)]

    def pack(arr):
        for k, (f, b) in enumerate(blocks()):
            for s in range(2):
                stage[arr, k * TOK : (k + 1) * TOK, s * LANES : (s + 1) * LANES] = rows_in[
                    arr, :, feature(f, s, b)
                ]
        packed = reorder(p_grp[...], stage[arr])
        for s in range(2):
            zsend[2 * arr + s] = packed[:, s * LANES : (s + 1) * LANES].reshape(NZ, BLK * CAP_G, LANES)

    def send(src, dst, s_sem, r_sem, device):
        pltpu.make_async_remote_copy(
            src_ref=src, dst_ref=dst, send_sem=s_sem, recv_sem=r_sem, device_id=device, device_id_type=MESH
        ).start()

    def start_z(src, dst, s_sem, r_sem):
        for z in z_peers:
            send(src.at[z], dst.at[node], s_sem, r_sem, (z, local))
        pltpu.make_async_copy(src.at[node], dst.at[node], r_sem).start()

    def start_y(src, dst, s_sem, r_sem):
        for y in y_peers:
            send(src.at[y], dst.at[my_y], s_sem, r_sem, place(y, my_x))
        pltpu.make_async_copy(src.at[my_y], dst.at[my_y], r_sem).start()

    def start_x(src_of, dst, s_sem, r_sem):
        for x in x_peers:
            send(src_of(x), dst.at[my_x], s_sem, r_sem, place(my_y, x))
        pltpu.make_async_copy(src_of(my_x), dst.at[my_x], r_sem).start()

    load_x.wait()
    pack(0)
    pl.semaphore_wait(barrier, NZ - 1 + NY - 1 + NX - 1 + 1)
    for k in range(2):
        start_z(zsend.at[k], zrecv.at[k], zs_sem.at[k], zr_sem.at[k])
    load_y.wait()
    pack(1)
    for k in range(2, 4):
        start_z(zsend.at[k], zrecv.at[k], zs_sem.at[k], zr_sem.at[k])

    keep = pl.multiple_of(my_h * QUART, QUART)
    other = pl.multiple_of(QUART - my_h * QUART, QUART)
    weights = (wg_hbm, wu_hbm, wd_hbm)
    kept = [
        pltpu.make_async_copy(
            w.at[:, pl.ds(keep, QUART)], wbuf.at[m, core, :, pl.ds(keep, QUART)], wa_sem.at[m]
        )
        for m, w in enumerate(weights)
    ]
    swapped = [
        pltpu.make_async_remote_copy(
            src_ref=w.at[:, pl.ds(other, QUART)], dst_ref=wbuf.at[m, core, :, pl.ds(keep, QUART)],
            send_sem=wo_sem.at[m], recv_sem=wb_sem.at[m],
            device_id=place(my_y, lax.rem(my_x + 2, NX)), device_id_type=MESH,
        )
        for m, w in enumerate(weights)
    ]
    for m, w in enumerate(weights):
        kept[m].start()

        @pl.when(my_k == 0)
        def _():
            pltpu.make_async_copy(
                w.at[:, pl.ds(other, QUART)], wbuf.at[m, core, :, pl.ds(other, QUART)], wb_sem.at[m]
            ).start()

        @pl.when(my_k == 1)
        def _():
            swapped[m].start()

    twins = [
        pltpu.make_async_remote_copy(
            src_ref=wbuf.at[m, core], dst_ref=wbuf.at[m, core], send_sem=ws_sem.at[m], recv_sem=wr_sem.at[m],
            device_id=twin, device_id_type=MESH,
        )
        for m in range(3)
    ]

    small[1].wait()
    small[2].wait()
    picks_lane = picks_ref[...].astype(F32)
    picks = column(picks_lane, TOK)
    row48 = lax.broadcasted_iota(I32, (TOK, TOK), 0)
    col48 = lax.broadcasted_iota(I32, (TOK, TOK), 1)
    same = (picks == picks_lane) & (col48 < row48)
    rank = jnp.sum(jnp.where(same, 1.0, 0.0), axis=1, keepdims=True)
    grp_n, grp_k, grp_c = lax.div(lane, BLK * CAP_G), lax.rem(lax.div(lane, CAP_G), BLK), lax.rem(lane, CAP_G)
    grp_row = grp_n * CAP_G + grp_c
    slot_key = spread(picks * (BLK * CAP_E) + rank, grp_row).astype(I32) + grp_k * CAP_E
    gate = spread(column(gates_ref[...].astype(F32), TOK), grp_row)
    p_exp[...] = one_hot(slot_key)
    rows2d = lax.broadcasted_iota(I32, (ROWS, ROWS), 0)
    p_expw[...] = jnp.where(rows2d == slot_key, gate, 0.0).astype(BF16)
    exp_e, exp_k, exp_r = (
        lax.div(lane, BLK * CAP_E), lax.rem(lax.div(lane, CAP_E), BLK), lax.rem(lane, CAP_E),
    )
    p_mat[...] = one_hot(exp_k * TOK + exp_e * CAP_E + exp_r)
    mat_k, mat_y, mat_r = (
        lax.div(lane, TOK), lax.div(lax.rem(lane, TOK), CAP_E), lax.rem(lane, CAP_E),
    )
    p_mat_t[...] = one_hot(mat_y * (BLK * CAP_E) + mat_k * CAP_E + mat_r)
    row_id = lax.broadcasted_iota(I32, (TOK, ROWS), 0).astype(F32)
    wanted = (exp_e * CAP_E + exp_r).astype(F32)
    source = jnp.sum(
        jnp.where(picks * CAP_E + rank == wanted, row_id, 0.0), axis=0, keepdims=True
    ).astype(I32)
    p_exp_t[...] = one_hot(
        lax.div(source, CAP_G) * (BLK * CAP_G) + exp_k * CAP_G + lax.rem(source, CAP_G)
    )
    turn_id = lax.broadcasted_iota(I32, (16, ROWS), 0)
    at_group = (order == grp_n.astype(F32)) & (turn_id < NZ)
    position = jnp.sum(
        jnp.where(at_group, turn_id.astype(F32), 0.0), axis=0, keepdims=True
    ).astype(I32)
    p_grp_t[...] = one_hot(grp_k * TOK + grp_c * NZ + position)

    def dispatch(k, matrix):
        drain(zrecv.at[k], zr_sem.at[k])
        ysend[k] = reorder(matrix[...], zrecv[k].reshape(ROWS, LANES)).reshape(NY, BLK * CAP_E, LANES)
        start_y(ysend.at[k], yrecv.at[k], ys_sem.at[k], yr_sem.at[k])

    def forward(k):
        drain(yrecv.at[k], yr_sem.at[k])
        xsend[k] = reorder(p_mat[...], yrecv[k].reshape(ROWS, LANES)).reshape(2, FB * TOK, LANES)
        start_x(lambda x: xsend.at[k, lax.rem(x, 2)], xrecv.at[k], xs_sem.at[k], xr_sem.at[k])

    def collect(k):
        drain(xrecv.at[k], xr_sem.at[k])
        for x in range(NX):
            for b in range(FB):
                lhs[k, x * TOK : (x + 1) * TOK, b * LANES : (b + 1) * LANES] = xrecv[
                    k, x, b * TOK : (b + 1) * TOK, :
                ]

    def product(k, m):
        return jnp.dot(lhs[k], wbuf[m, k % 2], preferred_element_type=F32)

    def hand_over(m):
        for j in range(2):
            part_out[m, j] = part[m, :, j * QUART : (j + 1) * QUART].astype(BF16)
            send(
                part_out.at[m, j], part_in.at[m, my_h], ps_sem.at[m], pr_sem.at[m],
                place(my_y, 2 * j + 1 - my_k),
            )

    def whole(m):
        drain(part_in.at[m], pr_sem.at[m])
        return part[m] + jnp.concatenate([part_in[m, 0], part_in[m, 1]], axis=1).astype(F32)

    dispatch(0, p_exp)
    dispatch(1, p_exp)
    forward(0)
    dispatch(2, p_expw)
    forward(1)
    dispatch(3, p_expw)
    for m in range(3):
        kept[m].wait()
        drain(wbuf.at[m, core, :, pl.ds(other, QUART)], wb_sem.at[m])
        twins[m].start()
    forward(2)
    for m in range(3):
        twins[m].wait_recv()
    collect(0)
    for m in range(2):
        part[m] = product(0, m)
    collect(1)
    for m in range(2):
        part[m] += product(1, m)
        hand_over(m)
    forward(3)
    collect(2)
    part[2] = product(2, 2)
    collect(3)
    part[2] += product(3, 2)
    hand_over(2)

    pre_gate = whole(0)
    pre_up = whole(1)
    sig = jax.nn.sigmoid(pre_gate)
    gate_factor = pre_up * sig * (1.0 + pre_gate * (1.0 - sig))
    up_factor = pre_gate * sig
    grad_hid = whole(2)
    d_gate = (grad_hid * gate_factor).astype(BF16)
    d_up = (grad_hid * up_factor).astype(BF16)
    dims = (((1,), (1,)), ((), ()))
    for s in range(2):
        contrib = lax.dot_general(d_gate, wbuf[0, s], dims, preferred_element_type=F32)
        contrib = contrib + lax.dot_general(d_up, wbuf[1, s], dims, preferred_element_type=F32)
        contrib = contrib.astype(BF16)
        for x in range(NX):
            for b in range(FB):
                rsend[s, x, b * TOK : (b + 1) * TOK, :] = contrib[
                    x * TOK : (x + 1) * TOK, b * LANES : (b + 1) * LANES
                ]
        start_x(lambda x: rsend.at[s, x], rrecv.at[s], rs_sem.at[s], rr_sem.at[s])

    for s in range(2):
        drain(rrecv.at[s], rr_sem.at[s])
        summed = [(rrecv[s, f].astype(F32) + rrecv[s, f + 2].astype(F32)).astype(BF16) for f in range(2)]
        qsend[s] = reorder(p_mat_t[...], jnp.concatenate(summed, axis=0)).reshape(NY, BLK * CAP_E, LANES)
        start_y(qsend.at[s], qrecv.at[s], qs_sem.at[s], qr_sem.at[s])
    for s in range(2):
        drain(qrecv.at[s], qr_sem.at[s])
        bsend[s] = reorder(p_exp_t[...], qrecv[s].reshape(ROWS, LANES)).reshape(NZ, BLK * CAP_G, LANES)
        start_z(bsend.at[s], brecv.at[s], bs_sem.at[s], br_sem.at[s])
    for s in range(2):
        drain(brecv.at[s], br_sem.at[s])
        result = reorder(p_grp_t[...], brecv[s].reshape(ROWS, LANES))
        for k, (f, b) in enumerate(blocks()):
            out_ref[:, feature(f, s, b)] = result[k * TOK : (k + 1) * TOK, :]

    for k in range(4):
        drain(zsend.at[k, pl.ds(0, NZ - 1)], zs_sem.at[k])
        drain(ysend.at[k, pl.ds(0, NY - 1)], ys_sem.at[k])
        drain(xrecv.at[k, pl.ds(0, NX - 1)], xs_sem.at[k])
    for s in range(2):
        drain(rsend.at[s, pl.ds(0, NX - 1)], rs_sem.at[s])
        drain(qsend.at[s, pl.ds(0, NY - 1)], qs_sem.at[s])
        drain(bsend.at[s, pl.ds(0, NZ - 1)], bs_sem.at[s])
    for m in range(3):
        drain(part_out.at[m], ps_sem.at[m])
        twins[m].wait_send()

        @pl.when(my_k == 1)
        def _():
            swapped[m].wait_send()


def per_device(inputs_x, grad_out, group_order, route_picks, gate_weights, w_gate, w_up, w_down):
    hbm = pl.BlockSpec(memory_space=pltpu.HBM)
    square = pltpu.VMEM((ROWS, ROWS), BF16)
    dma = pltpu.SemaphoreType.DMA
    z_buf, y_buf, x_buf = (NZ, BLK * CAP_G, LANES), (NY, BLK * CAP_E, LANES), (NX, FB * TOK, LANES)
    return pl.pallas_call(
        kernel,
        out_shape=jax.ShapeDtypeStruct(inputs_x.shape, BF16),
        in_specs=[hbm] * 8,
        out_specs=pl.BlockSpec(memory_space=pltpu.VMEM),
        scratch_shapes=[
            pltpu.VMEM((1, NZ), I32),
            pltpu.VMEM((1, TOK), I32),
            pltpu.VMEM((1, TOK), BF16),
            pltpu.VMEM((2, TOK, 4 * HALF), BF16),
            pltpu.VMEM((2, ROWS, 2 * LANES), BF16),
            pltpu.VMEM((4, *z_buf), BF16),
            pltpu.VMEM((4, *z_buf), BF16),
            pltpu.VMEM((4, *y_buf), BF16),
            pltpu.VMEM((4, *y_buf), BF16),
            pltpu.VMEM((4, 2, FB * TOK, LANES), BF16),
            pltpu.VMEM((4, *x_buf), BF16),
            pltpu.VMEM((4, NX * TOK, HALF), BF16),
            pltpu.VMEM((3, 2, HALF, HALF), BF16),
            pltpu.VMEM((3, NX * TOK, HALF), F32),
            pltpu.VMEM((3, 2, NX * TOK, QUART), BF16),
            pltpu.VMEM((3, 2, NX * TOK, QUART), BF16),
            pltpu.VMEM((2, *x_buf), BF16),
            pltpu.VMEM((2, *x_buf), BF16),
            pltpu.VMEM((2, *y_buf), BF16),
            pltpu.VMEM((2, *y_buf), BF16),
            pltpu.VMEM((2, *z_buf), BF16),
            pltpu.VMEM((2, *z_buf), BF16),
            square, square, square, square, square, square, square,
            dma((5,)), dma((3,)), dma((3,)), dma((3,)), dma((3,)), dma((3,)),
            dma((4,)), dma((4,)), dma((4,)), dma((4,)), dma((4,)), dma((4,)),
            dma((3,)), dma((3,)), dma((2,)), dma((2,)), dma((2,)), dma((2,)), dma((2,)), dma((2,)),
        ],
        compiler_params=pltpu.CompilerParams(
            collective_id=0, has_side_effects=True, vmem_limit_bytes=60 * 2**20
        ),
    )(
        group_order, route_picks.reshape(1, TOK), gate_weights.reshape(1, TOK), inputs_x, grad_out,
        w_gate, w_up, w_down,
    )


def solution(mesh):
    placed = P(("node", "local"), None)
    return jax.shard_map(
        per_device, mesh=mesh, in_specs=(placed,) * 8, out_specs=placed, check_vma=False
    )
```

time: 173 us -> 77.2 us (0.45)
  Pallas kernels: 0 us -> 75.1 us
  waiting for transfers between devices: 67 us -> 0 us
  blocking collectives: 36.7 us -> 0 us
  starting transfers between devices: 35.3 us -> 0 us
  other arithmetic: 13.9 us -> 0 us
  local copies, waits for them, and re-layouts: 14 us -> 1.62 us
  matrix products: 3.71 us -> 0 us
    pallas_call x0 -> x1, Pallas kernels: none -> 75.1 us  [per_device(): pl.pallas_call(kernel, out_shape=jax.ShapeDtypeStruct(inputs_x.shape, BF1...]
    all_to_all x2 -> x0, waiting for transfers between devices: 42.6 us -> none  [the longest x1 23.2 us: local_move(): lax.all_to_all(payload, 'local', split_axis=1, concat_axis=1, tiled=True)]
    all_to_all x2 -> x0, blocking collectives: 36.7 us -> none  [the longest x1 20.4 us: local_move(): lax.all_to_all(payload, 'local', split_axis=1, concat_axis=1, tiled=True)]
    all_to_all x2 -> x0, starting transfers between devices: 25.8 us -> none  [the longest x1 15.2 us: node_move(): lax.all_to_all(payload, 'node', split_axis=1, concat_axis=1, tiled=True)]
    ppermute x4 -> x0, waiting for transfers between devices: 24.4 us -> none  [from_partner(): return lax.ppermute(value, axis, pairs)]
    ppermute x4 -> x0, starting transfers between devices: 9.51 us -> none  [from_partner(): return lax.ppermute(value, axis, pairs)]
    unnamed x2 -> x0, other arithmetic: 4.78 us -> none
    dot_general x9 -> x0, matrix products: 3.71 us -> none  [the longest x1 0.92 us: per_device(): jnp.dot(collect, arrived_home[0], preferred_element_type=jnp.float32)]
  transfers between devices with their start and end apart: 6 -> 0, of which waited for: 6 -> 0; matrix products, arithmetic and copies ran while one was open for 0% -> 0% of each run, Pallas kernels for 0% -> 0%
where the time goes in v2:
time: 77.2 us; the launch traced here: 76.7 us
  Pallas kernels  75.1 us (97%)
  local copies, waits for them, and re-layouts  1.62 us (2%)
    pallas_call x1, Pallas kernels, per_device(): pl.pallas_call(kernel, out_shape=jax.ShapeDtypeStruct(inputs_x.shape, BF1...  75.1 us
    unnamed x1, local copies, waits for them, and re-layouts  1.62 us

profile of v2, /device:TPU:6, one launch (start us, length us, event | category | flops | bytes accessed | tf_op | source)
XLA Modules:
  0.0 76.7 jit_solution(2712784509527025389)
XLA Ops:
  0.0 75.1 %shard_map.82 = bf16[48,2048]{1,0:T(8,128)(2,1)} custom-call(s32[1,12]{1,0:T(1,128)} %order_hbm.1, s32[1,48]{1,0:T(1,128)} %bitcast.2, bf16[1,48]{1,0:T(2,128)(2,1)} %bitcast.3, bf16[48,2048]{1,0:T(8,128)(2,1)} %x_hbm.1, bf16[48,2048]{1,0:T(8,128)(2,1)} %y_hbm.1, bf16[512,512]{1,0:T(8,128)(2,1)} %wg_hbm.1, bf16[512,512]{1,0:T(8,128)(2,1)} %wu_hbm.1, ...), custom_call_target="tpu_custom_call" | custom-call | tf_op jit(solution)/shard_map/pallas_call | solution.py:346
  75.1 1.6 %copy.10 = bf16[48,2048]{1,0:T(8,128)(2,1)} copy(bf16[48,2048]{1,0:T(8,128)(2,1)} %shard_map.82) | data formatting | bytes 393216

commit v3 on v2

--- a/solution.py
+++ b/solution.py
@@ -69,6 +69,19 @@
     x_peers = [lax.rem(my_x + step, NX) for step in (2, 1, 3)]
     twin = (node, local + 1 - 2 * core)
 
+    barrier = pltpu.get_barrier_semaphore()
+
+    def greet(device):
+        pl.semaphore_signal(barrier, inc=1, device_id=device, device_id_type=MESH)
+
+    for z in z_peers:
+        greet((z, local))
+    for y in y_peers:
+        greet(place(y, my_x))
+    for x in x_peers:
+        greet(place(my_y, x))
+    greet(twin)
+
     load_x = pltpu.make_async_copy(x_hbm, rows_in.at[0], in_sem.at[0])
     load_y = pltpu.make_async_copy(y_hbm, rows_in.at[1], in_sem.at[1])
     small = [
@@ -83,19 +96,6 @@
     small[1].start()
     small[2].start()
 
-    barrier = pltpu.get_barrier_semaphore()
-
-    def greet(device):
-        pl.semaphore_signal(barrier, inc=1, device_id=device, device_id_type=MESH)
-
-    for z in z_peers:
-        greet((z, local))
-    for y in y_peers:
-        greet(place(y, my_x))
-    for x in x_peers:
-        greet(place(my_y, x))
-    greet(twin)
-
     lane = lax.broadcasted_iota(I32, (1, ROWS), 1)
     tok_k, tok_t = lax.div(lane, TOK), lax.rem(lane, TOK)
     small[0].wait()
@@ -142,11 +142,12 @@
 
     load_x.wait()
     pack(0)
-    pl.semaphore_wait(barrier, NZ - 1 + NY - 1 + NX - 1 + 1)
-    for k in range(2):
-        start_z(zsend.at[k], zrecv.at[k], zs_sem.at[k], zr_sem.at[k])
     load_y.wait()
     pack(1)
+    pl.semaphore_wait(barrier, NZ - 1 + NY - 1 + NX - 1 + 1)
+    for z in z_peers:
+        send(zsend.at[pl.ds(0, 2), z], zrecv.at[pl.ds(0, 2), node], zs_sem.at[0], zr_sem.at[0], (z, local))
+    pltpu.make_async_copy(zsend.at[pl.ds(0, 2), node], zrecv.at[pl.ds(0, 2), node], zr_sem.at[0]).start()
     for k in range(2, 4):
         start_z(zsend.at[k], zrecv.at[k], zs_sem.at[k], zr_sem.at[k])
 
@@ -227,7 +228,8 @@
     p_grp_t[...] = one_hot(grp_k * TOK + grp_c * NZ + position)
 
     def dispatch(k, matrix):
-        drain(zrecv.at[k], zr_sem.at[k])
+        if k > 1:
+            drain(zrecv.at[k], zr_sem.at[k])
         ysend[k] = reorder(matrix[...], zrecv[k].reshape(ROWS, LANES)).reshape(NY, BLK * CAP_E, LANES)
         start_y(ysend.at[k], yrecv.at[k], ys_sem.at[k], yr_sem.at[k])
 
@@ -259,6 +261,7 @@
         drain(part_in.at[m], pr_sem.at[m])
         return part[m] + jnp.concatenate([part_in[m, 0], part_in[m, 1]], axis=1).astype(F32)
 
+    drain(zrecv.at[pl.ds(0, 2)], zr_sem.at[0])
     dispatch(0, p_exp)
     dispatch(1, p_exp)
     forward(0)
@@ -276,10 +279,11 @@
     for m in range(2):
         part[m] = product(0, m)
     collect(1)
-    for m in range(2):
-        part[m] += product(1, m)
-        hand_over(m)
+    part[0] += product(1, 0)
+    hand_over(0)
     forward(3)
+    part[1] += product(1, 1)
+    hand_over(1)
     collect(2)
     part[2] = product(2, 2)
     collect(3)
@@ -321,8 +325,10 @@
         for k, (f, b) in enumerate(blocks()):
             out_ref[:, feature(f, s, b)] = result[k * TOK : (k + 1) * TOK, :]
 
+    drain(zsend.at[pl.ds(0, 2), pl.ds(0, NZ - 1)], zs_sem.at[0])
     for k in range(4):
-        drain(zsend.at[k, pl.ds(0, NZ - 1)], zs_sem.at[k])
+        if k > 1:
+            drain(zsend.at[k, pl.ds(0, NZ - 1)], zs_sem.at[k])
         drain(ysend.at[k, pl.ds(0, NY - 1)], ys_sem.at[k])
         drain(xrecv.at[k, pl.ds(0, NX - 1)], xs_sem.at[k])
     for s in range(2):

time: 77.2 us -> 74.5 us (0.965)
  Pallas kernels: 75.1 us -> 72.4 us
    pallas_call x1, Pallas kernels: 75.1 us -> 72.4 us  [per_device(): pl.pallas_call(kernel, out_shape=jax.ShapeDtypeStruct(inputs_x.shape, BF1...]
where the time goes in v3:
time: 74.5 us; the launch traced here: 74 us
  Pallas kernels  72.4 us (97%)
  local copies, waits for them, and re-layouts  1.62 us (2%)
    pallas_call x1, Pallas kernels, per_device(): pl.pallas_call(kernel, out_shape=jax.ShapeDtypeStruct(inputs_x.shape, BF1...  72.4 us
    unnamed x1, local copies, waits for them, and re-layouts  1.62 us

profile of v3, /device:TPU:6, one launch (start us, length us, event | category | flops | bytes accessed | tf_op | source)
XLA Modules:
  0.0 74.0 jit_solution(1849507831507889204)
XLA Ops:
  0.0 72.4 %shard_map.82 = bf16[48,2048]{1,0:T(8,128)(2,1)} custom-call(s32[1,12]{1,0:T(1,128)} %order_hbm.1, s32[1,48]{1,0:T(1,128)} %bitcast.2, bf16[1,48]{1,0:T(2,128)(2,1)} %bitcast.3, bf16[48,2048]{1,0:T(8,128)(2,1)} %x_hbm.1, bf16[48,2048]{1,0:T(8,128)(2,1)} %y_hbm.1, bf16[512,512]{1,0:T(8,128)(2,1)} %wg_hbm.1, bf16[512,512]{1,0:T(8,128)(2,1)} %wu_hbm.1, ...), custom_call_target="tpu_custom_call" | custom-call | tf_op jit(solution)/shard_map/pallas_call | solution.py:352
  72.4 1.6 %copy.10 = bf16[48,2048]{1,0:T(8,128)(2,1)} copy(bf16[48,2048]{1,0:T(8,128)(2,1)} %shard_map.82) | data formatting | bytes 393216

commit v4 on v3

--- a/solution.py
+++ b/solution.py
@@ -319,12 +319,6 @@
         drain(qrecv.at[s], qr_sem.at[s])
         bsend[s] = reorder(p_exp_t[...], qrecv[s].reshape(ROWS, LANES)).reshape(NZ, BLK * CAP_G, LANES)
         start_z(bsend.at[s], brecv.at[s], bs_sem.at[s], br_sem.at[s])
-    for s in range(2):
-        drain(brecv.at[s], br_sem.at[s])
-        result = reorder(p_grp_t[...], brecv[s].reshape(ROWS, LANES))
-        for k, (f, b) in enumerate(blocks()):
-            out_ref[:, feature(f, s, b)] = result[k * TOK : (k + 1) * TOK, :]
-
     drain(zsend.at[pl.ds(0, 2), pl.ds(0, NZ - 1)], zs_sem.at[0])
     for k in range(4):
         if k > 1:
@@ -334,7 +328,6 @@
     for s in range(2):
         drain(rsend.at[s, pl.ds(0, NX - 1)], rs_sem.at[s])
         drain(qsend.at[s, pl.ds(0, NY - 1)], qs_sem.at[s])
-        drain(bsend.at[s, pl.ds(0, NZ - 1)], bs_sem.at[s])
     for m in range(3):
         drain(part_out.at[m], ps_sem.at[m])
         twins[m].wait_send()
@@ -342,6 +335,13 @@
         @pl.when(my_k == 1)
         def _():
             swapped[m].wait_send()
+    for s in range(2):
+        drain(brecv.at[s], br_sem.at[s])
+        result = reorder(p_grp_t[...], brecv[s].reshape(ROWS, LANES))
+        for k, (f, b) in enumerate(blocks()):
+            out_ref[:, feature(f, s, b)] = result[k * TOK : (k + 1) * TOK, :]
+    for s in range(2):
+        drain(bsend.at[s, pl.ds(0, NZ - 1)], bs_sem.at[s])
 
 
 def per_device(inputs_x, grad_out, group_order, route_picks, gate_weights, w_gate, w_up, w_down):
@@ -383,7 +383,7 @@
             dma((3,)), dma((3,)), dma((2,)), dma((2,)), dma((2,)), dma((2,)), dma((2,)), dma((2,)),
         ],
         compiler_params=pltpu.CompilerParams(
-            collective_id=0, has_side_effects=True, vmem_limit_bytes=60 * 2**20
+            collective_id=0, has_side_effects=True, vmem_limit_bytes=54886 * 2**10
         ),
     )(
         group_order, route_picks.reshape(1, TOK), gate_weights.reshape(1, TOK), inputs_x, grad_out,

time: 74.5 us -> 73.4 us (0.985)
  Pallas kernels: 72.4 us -> 71.6 us
    pallas_call x1, Pallas kernels: 72.4 us -> 71.6 us  [per_device(): pl.pallas_call(kernel, out_shape=jax.ShapeDtypeStruct(inputs_x.shape, BF1...]
    unnamed x1 -> x7, local copies, waits for them, and re-layouts: 1.62 us -> 1.36 us
where the time goes in v4:
time: 73.4 us; the launch traced here: 73 us
  Pallas kernels  71.6 us (98%)
  local copies, waits for them, and re-layouts  1.36 us (2%)
    pallas_call x1, Pallas kernels, per_device(): pl.pallas_call(kernel, out_shape=jax.ShapeDtypeStruct(inputs_x.shape, BF1...  71.6 us

profile of v4, /device:TPU:6, one launch (start us, length us, event | category | flops | bytes accessed | tf_op | source)
XLA Modules:
  0.0 73.0 jit_solution(1075990137515190111)
XLA Ops:
  0.0 0.0 copy-start
  0.0 0.0 copy-start.1
  0.0 0.0 copy-start.2
  0.0 0.6 copy-done
  0.7 0.0 copy-done.1
  0.7 0.0 copy-done.2
  0.7 71.6 %shard_map.82 = bf16[48,2048]{1,0:T(8,128)(2,1)S(1)} custom-call(s32[1,12]{1,0:T(1,128)S(1)} %copy-done, s32[1,48]{1,0:T(1,128)S(1)} %bitcast.2, bf16[1,48]{1,0:T(2,128)(2,1)S(1)} %bitcast.3, bf16[48,2048]{1,0:T(8,128)(2,1)} %x_hbm.1, bf16[48,2048]{1,0:T(8,128)(2,1)} %y_hbm.1, bf16[512,512]{1,0:T(8,128)(2,1)} %wg_hbm.1, bf16[512,512]{1,0:T(8,128)(2,1)} %wu_hbm.1, ...), custom_call_target="tpu_custom_call" | custom-call | tf_op jit(solution)/shard_map/pallas_call | solution.py:352
  72.3 0.7 copy.10
Async XLA Ops:
  0.0 0.7 copy-start
  0.0 0.7 copy-start.1
  0.0 0.7 copy-start.2

commit v5 on v4

--- a/solution.py
+++ b/solution.py
@@ -249,13 +249,16 @@
     def product(k, m):
         return jnp.dot(lhs[k], wbuf[m, k % 2], preferred_element_type=F32)
 
-    def hand_over(m):
+    def hand_over(k, m):
         for j in range(2):
-            part_out[m, j] = part[m, :, j * QUART : (j + 1) * QUART].astype(BF16)
+            half = slice(j * QUART, (j + 1) * QUART)
+            value = part[m, :, half] + jnp.dot(lhs[k], wbuf[m, k % 2, :, half], preferred_element_type=F32)
+            part_out[m, j] = value.astype(BF16)
             send(
                 part_out.at[m, j], part_in.at[m, my_h], ps_sem.at[m], pr_sem.at[m],
                 place(my_y, 2 * j + 1 - my_k),
             )
+            part[m, :, half] = value
 
     def whole(m):
         drain(part_in.at[m], pr_sem.at[m])
@@ -279,16 +282,13 @@
     for m in range(2):
         part[m] = product(0, m)
     collect(1)
-    part[0] += product(1, 0)
-    hand_over(0)
+    hand_over(1, 0)
     forward(3)
-    part[1] += product(1, 1)
-    hand_over(1)
+    hand_over(1, 1)
     collect(2)
     part[2] = product(2, 2)
     collect(3)
-    part[2] += product(3, 2)
-    hand_over(2)
+    hand_over(3, 2)
 
     pre_gate = whole(0)
     pre_up = whole(1)

time: 73.4 us -> 74 us (level)
  no operation moved by 1% of the time
where the time goes in v5:
time: 74 us; the launch traced here: 73.3 us
  Pallas kernels  71.9 us (97%)
  local copies, waits for them, and re-layouts  1.36 us (2%)
    pallas_call x1, Pallas kernels, per_device(): pl.pallas_call(kernel, out_shape=jax.ShapeDtypeStruct(inputs_x.shape, BF1...  71.9 us

profile of v5, /device:TPU:6, one launch (start us, length us, event | category | flops | bytes accessed | tf_op | source)
XLA Modules:
  0.0 73.3 jit_solution(750561039915402972)
XLA Ops:
  0.0 0.0 copy-start
  0.0 0.0 copy-start.1
  0.0 0.0 copy-start.2
  0.0 0.6 copy-done
  0.7 0.0 copy-done.1
  0.7 0.0 copy-done.2
  0.7 71.9 %shard_map.82 = bf16[48,2048]{1,0:T(8,128)(2,1)S(1)} custom-call(s32[1,12]{1,0:T(1,128)S(1)} %copy-done, s32[1,48]{1,0:T(1,128)S(1)} %bitcast.2, bf16[1,48]{1,0:T(2,128)(2,1)S(1)} %bitcast.3, bf16[48,2048]{1,0:T(8,128)(2,1)} %x_hbm.1, bf16[48,2048]{1,0:T(8,128)(2,1)} %y_hbm.1, bf16[512,512]{1,0:T(8,128)(2,1)} %wg_hbm.1, bf16[512,512]{1,0:T(8,128)(2,1)} %wu_hbm.1, ...), custom_call_target="tpu_custom_call" | custom-call | tf_op jit(solution)/shard_map/pallas_call | solution.py:352
  72.6 0.7 copy.10
Async XLA Ops:
  0.0 0.7 copy-start
  0.0 0.7 copy-start.1
  0.0 0.7 copy-start.2
